TPU v7x, 512 devices: a whole 4x8x8 slice. The times are simulated.
512 devices in a mesh: fsdp: 64 (over y, z_hi, x), tp: 8 (over z_lo, core).
Axes of the slice: x: 4, y: 8, z: 8 (z_hi: 2, z_lo: 4; z = z_hi * 4 + z_lo), core: 2. Of those that a mesh axis runs over, the one named last changes fastest.
Arguments:
- decode_row_inputs: bfloat16 [3, 512, 8192], P(None, 'fsdp'), may hold values from -6 to 6
- lengths: int32 [512], P('fsdp'), may hold values from 2 to 64, as said below
- queries: bfloat16 [3, 512, 8192], P(None, 'fsdp', 'tp'), may hold values from -6 to 6
- rotated_key_cache: bfloat16 [512, 64, 1024], P('fsdp', None, 'tp'), may hold values from -6 to 6
- value_cache_rows: bfloat16 [512, 64, 1024], P('fsdp', None, 'tp'), may hold values from -6 to 6
- key_value_weight: bfloat16 [2, 8192, 1024], P(None, None, 'tp'), may hold values from -0.0625 to 0.0625
- key_value_bias: bfloat16 [2, 1024], P(None, 'tp'), may hold values from -3 to 3
- adapter_down_weight: bfloat16 [8192, 128], P(('fsdp', 'tp')), may hold values from -0.0625 to 0.0625
- adapter_up_weight: bfloat16 [2, 64, 1024], P(None, 'fsdp', 'tp'), may hold values from -0.75 to 0.75
Outputs:
- attended: bfloat16 [3, 512, 8192], P(None, 'fsdp', 'tp')
- new_entries: bfloat16 [2, 3, 512, 1024], P(None, None, 'fsdp', 'tp')
Inputs may be any that keep to these rules, and one draw needn't show every extreme that they name: `lengths`: the first row of every aligned block of 8 rows holds 64 cached tokens.
All inputs are finite; a program needn't handle non-finite values.
Results may differ from a plain program's by a relative error of at most 0.0075.
Values may be sent and summed in bfloat16 or wider, within the bound.
A program may use at most 64 MiB of HBM per device.

v0:
```python
import jax
import jax.numpy as jnp
from jax import lax
from jax.sharding import PartitionSpec as P

HEADS = 64
KEY_VALUE_HEADS = 8
HEAD_SIZE = 128


ADAPTER_SCALE = 2.0
ROPE_BASE = 1000000.0
MASKED = -1e30


def rotary(vectors, positions):
    half_size = vectors.shape[-1] // 2
    frequency = ROPE_BASE ** (-2.0 * jnp.arange(half_size, dtype=jnp.float32) / vectors.shape[-1])
    angle = positions[..., None] * frequency
    cosine = jnp.cos(angle)
    sine = jnp.sin(angle)
    lower = vectors[..., :half_size]
    upper = vectors[..., half_size:]
    return jnp.concatenate([lower * cosine - upper * sine, upper * cosine + lower * sine], axis=-1)


def body(
    decode_row_inputs,
    lengths,
    queries,
    rotated_key_cache,
    value_cache_rows,
    key_value_weight,
    key_value_bias,
    adapter_down_weight,
    adapter_up_weight,
):
    gathered_up_weight = lax.all_gather(adapter_up_weight, "fsdp", axis=1, tiled=True)
    rank_size = gathered_up_weight.shape[1]
    steps, rows, width = decode_row_inputs.shape
    columns = key_value_weight.shape[2]
    flattened = decode_row_inputs.reshape(steps * rows, width)
    shard_portion = lax.all_gather(adapter_down_weight, ("fsdp", "tp"), axis=0, tiled=True)
    key_weight_change = jnp.dot(
        shard_portion[:, :rank_size], gathered_up_weight[0], preferred_element_type=jnp.float32
    )
    value_weight_change = jnp.dot(
        shard_portion[:, rank_size:], gathered_up_weight[1], preferred_element_type=jnp.float32
    )
    weight_update = jnp.stack([key_weight_change, value_weight_change])
    merged_weight = (key_value_weight.astype(jnp.float32) + ADAPTER_SCALE * weight_update).astype(
        jnp.bfloat16
    )
    kv_local = columns // HEAD_SIZE
    group = HEADS // KEY_VALUE_HEADS
    cache_slots = rotated_key_cache.shape[1]
    projected = jnp.einsum(
        "nd,kdc->knc", flattened, merged_weight, preferred_element_type=jnp.float32
    )
    projected = projected + key_value_bias.astype(jnp.float32)[:, None, :]
    positions = (lengths[None, :] + jnp.arange(steps, dtype=jnp.int32)[:, None]).astype(jnp.float32)
    fresh_keys = rotary(
        projected[0].reshape(steps, rows, kv_local, HEAD_SIZE), positions[:, :, None]
    ).astype(jnp.bfloat16)
    fresh_values = projected[1].reshape(steps, rows, kv_local, HEAD_SIZE).astype(jnp.bfloat16)
    scale_factor = HEAD_SIZE ** (-0.5)
    grouped_queries = queries.reshape(steps, rows, kv_local, group, HEAD_SIZE)
    stored_keys = rotated_key_cache.reshape(rows, cache_slots, kv_local, HEAD_SIZE)
    stored_values = value_cache_rows.reshape(rows, cache_slots, kv_local, HEAD_SIZE)
    cached_scores = (
        jnp.einsum(
            "sbkgd,blkd->sbkgl", grouped_queries, stored_keys, preferred_element_type=jnp.float32
        )
        * scale_factor
    )
    valid = jnp.arange(cache_slots, dtype=jnp.int32)[None, :] < lengths[:, None]
    cached_scores = jnp.where(valid[None, :, None, None, :], cached_scores, MASKED)
    fresh_scores = (
        jnp.einsum(
            "sbkgd,tbkd->sbkgt", grouped_queries, fresh_keys, preferred_element_type=jnp.float32
        )
        * scale_factor
    )
    causal = (
        jnp.arange(steps, dtype=jnp.int32)[None, :] <= jnp.arange(steps, dtype=jnp.int32)[:, None]
    )
    fresh_scores = jnp.where(causal[:, None, None, None, :], fresh_scores, MASKED)
    scores = jnp.concatenate([cached_scores, fresh_scores], axis=-1)
    peak = jnp.max(scores, axis=-1, keepdims=True)
    raised = jnp.exp(scores - peak)
    weights = (raised / jnp.sum(raised, axis=-1, keepdims=True)).astype(jnp.bfloat16)
    attended = jnp.einsum(
        "sbkgl,blkd->sbkgd",
        weights[..., :cache_slots],
        stored_values,
        preferred_element_type=jnp.float32,
    )
    attended = attended + jnp.einsum(
        "sbkgt,tbkd->sbkgd",
        weights[..., cache_slots:],
        fresh_values,
        preferred_element_type=jnp.float32,
    )
    attended = attended.astype(jnp.bfloat16).reshape(steps, rows, kv_local * group * HEAD_SIZE)
    entries = jnp.stack(
        [fresh_keys.reshape(steps, rows, columns), fresh_values.reshape(steps, rows, columns)]
    )
    return (attended, entries)


def solution(mesh):
    placed = (
        P(None, "fsdp", None),
        P("fsdp"),
        P(None, "fsdp", "tp"),
        P("fsdp", None, "tp"),
        P("fsdp", None, "tp"),
        P(None, None, "tp"),
        P(None, "tp"),
        P(("fsdp", "tp"), None),
        P(None, "fsdp", "tp"),
    )
    return jax.shard_map(
        body,
        mesh=mesh,
        in_specs=placed,
        out_specs=(P(None, "fsdp", "tp"), P(None, None, "fsdp", "tp")),
        check_vma=False,
    )
```

profile of v0, /device:TPU:1, one launch (start us, length us, event | category | flops | bytes accessed | tf_op | source)
XLA Modules:
  0.0 790.3 jit_solution(13327882372944158315)
XLA Ops:
  7.2 0.0 copy-start
  7.2 0.0 all-gather.2.cloned.1.call-start
  7.2 0.7 all-gather.2.cloned.1.call-update
  7.9 0.7 convert_element_type.68
  8.6 198.5 %all_gather.7 = bf16[2,64,128]{2,0,1:T(2,128)(2,1)S(1)} all-gather(bf16[2,1,128]{2,0,1:T(2,128)(2,1)} %param.17), channel_id=1, replica_groups=mesh['fsdp'=64,'tp'=8] {'fsdp'}, dimensions={1}, use_global_device_ids=true | all-gather | bytes 33280 | tf_op jit(solution)/shard_map/all_gather | solution.py:38
  207.1 0.7 iota_compare_fusion
  207.9 0.7 add_convert_fusion
  208.7 1.2 fusion.44
  209.8 564.8 %all-gather.2.cloned.1.call-done = bf16[8192,128]{1,0:T(8,128)(2,1)} async-done(((bf16[16,128]{1,0:T(8,128)(2,1)}), bf16[8192,128]{1,0:T(8,128)(2,1)}) %all-gather.2.cloned.1.call-update) | async-done | bytes 2097168 | tf_op jit(solution)/shard_map/all_gather | solution.py:43
  774.7 0.0 copy-start.1
  774.7 2.7 convolution_bitcast_fusion
  777.4 0.0 copy-start.4
  777.4 0.0 copy-done.1
  777.4 0.7 convolution_bitcast_fusion.1
  778.1 0.0 copy-done
  778.1 1.5 copy-done.4
  779.5 0.0 copy-start.2
  779.5 0.0 copy-start.3
  779.5 1.1 fusion.16
  780.7 0.1 fusion.43
  780.7 0.2 fusion.30
  780.9 0.0 copy-done.2
  781.0 0.3 fusion.45
  781.3 0.2 fusion.33
  781.5 0.2 divide_convert_fusion
  781.7 0.0 copy-done.3
  781.7 0.2 convolution_bitcast_fusion.2
  781.8 0.2 fusion.12
  782.1 0.6 reshape.256
  782.7 0.1 pad_maximum_fusion
  782.8 0.6 copy.43
  (8 shorter events, 0.1 us)
Async XLA Ops:
  7.2 770.9 %copy-start = (bf16[3,8,8192]{2,1,0:T(8,128)(2,1)S(1)}, bf16[3,8,8192]{2,1,0:T(8,128)(2,1)}, u32[]{:S(2)}) copy-start(bf16[3,8,8192]{2,1,0:T(8,128)(2,1)} %param.9) | copy-start | bytes 1179652
  7.2 767.5 %all-gather.2.cloned.1.call-start = ((), (), s32[]{:S(2)}) async-start(), calls=%async_computation | async-start | bytes 2101248 | tf_op jit(solution)/shard_map/all_gather | solution.py:43
  774.7 2.7 copy-start.1
  777.4 2.2 copy-start.4
  779.5 1.4 copy-start.2
  779.5 2.1 copy-start.3
Sparse Core Ops, SparseCore 0:
  10.1 764.4 all-gather.1
where the time goes:
time: 790 us
  waiting for transfers between devices  566 us (72%)
  blocking collectives  199 us (25%)
  between operations  14.1 us (2%)
    all_gather x1, waiting for transfers between devices, body(): lax.all_gather(adapter_down_weight, ('fsdp', 'tp'), axis=0, tiled=True)  565 us
    all_gather x1, blocking collectives, body(): lax.all_gather(adapter_up_weight, 'fsdp', axis=1, tiled=True)  199 us
  transfers between devices with their start and end apart: 1, of which 1 were waited for; matrix products, arithmetic and copies ran while one was open for 0% of the time, Pallas kernels for 0%

commit v1 on v0

v1 whole, which is shorter than its diff:
```python
import functools
import math

import jax
import jax.numpy as jnp
from jax import lax
from jax.experimental import pallas as pl
from jax.experimental.pallas import tpu as pltpu
from jax.sharding import PartitionSpec as P

HEAD = 128
GROUP = 8
STEPS = 3
ROWS = 8
CACHE = 64
NX = 4
ADAPTER_SCALE = 2.0
ROPE_BASE = 1000000.0
MASKED = -1e30
MESH = pl.DeviceIdType.MESH
F32 = jnp.float32
BF16 = jnp.bfloat16
N = STEPS * ROWS
M = STEPS * GROUP * ROWS
SLOTS = ROWS * CACHE
W_PARTS = 8


def iota(shape, dim):
    return lax.broadcasted_iota(jnp.int32, shape, dim)


def dot(a, b):
    return jnp.dot(a, b, preferred_element_type=F32)


def dot_t(a, b):
    return lax.dot_general(a, b, (((1,), (1,)), ((), ())), preferred_element_type=F32)


def stack_steps(ref, columns):
    return jnp.concatenate([ref[s, :, columns].astype(F32) for s in range(STEPS)], axis=0)


def kernel(
    nq,
    ntp,
    x_hbm,
    len_hbm,
    q_hbm,
    k_hbm,
    v_hbm,
    w_hbm,
    bias_hbm,
    d_hbm,
    u_hbm,
    att_hbm,
    ent_hbm,
    x_v,
    len_s,
    q_v,
    k_v,
    v_v,
    w_v,
    bias_v,
    u_v,
    d_all,
    xs,
    xr,
    u1,
    u2,
    pp,
    pr,
    pt,
    xb,
    proj,
    cos_v,
    sin_v,
    qb,
    peak_c,
    total_c,
    acc_c,
    ublk,
    att_v,
    ent_v,
    in_sem,
    w_sem,
    out_sem,
    d_send,
    d_recv,
    x_send,
    x_recv,
    u1_send,
    u1_recv,
    u2_send,
    u2_recv,
    p_send,
    p_recv,
    t_send,
    t_recv,
):
    f = lax.axis_index("fsdp")
    t = lax.axis_index("tp")
    q = f // NX
    x = lax.rem(f, NX)
    d_rows = d_all.shape[1]
    width = x_v.shape[2]

    loads = {}
    for i, (name, src, dst) in enumerate(
        [
            ("d", d_hbm, d_all.at[q]),
            ("u", u_hbm, u_v),
            ("x", x_hbm, x_v),
            ("len", len_hbm, len_s),
            ("bias", bias_hbm, bias_v),
            ("q", q_hbm, q_v),
            ("k", k_hbm, k_v),
            ("v", v_hbm, v_v),
        ]
    ):
        loads[name] = pltpu.make_async_copy(src, dst, in_sem.at[i])
        loads[name].start()
    part = width // W_PARTS

    def w_load(i):
        rows = pl.ds(pl.multiple_of(i * part, part), part)
        return pltpu.make_async_copy(w_hbm.at[:, rows], w_v.at[:, rows], w_sem.at[i])

    for i in range(W_PARTS):
        w_load(i).start()

    def at_q(d):
        return lax.rem(q + d, nq) * NX + x

    def at_x(d):
        return q * NX + lax.rem(x + d, NX)

    def at_t(d):
        return lax.rem(t + d, ntp)

    barrier = pltpu.get_barrier_semaphore()
    for d in range(1, nq):
        pl.semaphore_signal(barrier, inc=1, device_id=(at_q(d), t), device_id_type=MESH)
    for d in range(1, NX):
        pl.semaphore_signal(barrier, inc=1, device_id=(at_x(d), t), device_id_type=MESH)
    for d in range(1, ntp):
        pl.semaphore_signal(barrier, inc=1, device_id=(f, at_t(d)), device_id_type=MESH)

    loads["u"].wait()
    u1[q] = jnp.concatenate([u_v[0], u_v[1]], axis=1).astype(F32)
    span = ntp * d_rows
    per = HEAD // d_rows
    groups = nq // per
    pick = (
        lax.rem(iota((per * span, HEAD), 0), span)
        == t * d_rows + lax.rem(iota((per * span, HEAD), 1), d_rows)
    ) & (iota((per * span, HEAD), 0) // span == iota((per * span, HEAD), 1) // d_rows)
    pick = jnp.where(pick, 1.0, 0.0).astype(BF16)
    loads["x"].wait()
    rows = []
    for j in range(NX):
        for g in range(groups):
            rows.append(
                jnp.concatenate(
                    [
                        stack_steps(x_v, pl.ds(((g * per + i) * NX + j) * span, span))
                        for i in range(per)
                    ],
                    axis=1,
                )
            )
    picked = dot(jnp.concatenate(rows, axis=0).astype(BF16), pick)
    for j in range(NX):
        for g in range(groups):
            base = (j * groups + g) * N
            for s in range(STEPS):
                xs[j, s, :, g * HEAD : (g + 1) * HEAD] = picked[
                    base + s * ROWS : base + (s + 1) * ROWS
                ].astype(BF16)
    xr[x] = xs[x]
    loads["d"].wait()

    pl.semaphore_wait(barrier, nq - 1 + NX - 1 + ntp - 1)

    def remote(src, dst, send, recv, where):
        return pltpu.make_async_remote_copy(
            src_ref=src, dst_ref=dst, send_sem=send, recv_sem=recv, device_id=where, device_id_type=MESH
        )

    def from_q(d):
        return lax.rem(q + nq - d, nq)

    def from_x(d):
        return lax.rem(x + NX - d, NX)

    def from_t(d):
        return lax.rem(t + ntp - d, ntp)

    def d_copy(d, block):
        return remote(d_all.at[block], d_all.at[block], d_send.at[d], d_recv.at[d], (at_q(d), t))

    def u1_copy(d, block):
        return remote(u1.at[block], u1.at[block], u1_send.at[d], u1_recv.at[d], (at_q(d), t))

    def x_copy(d, block):
        return remote(xs.at[lax.rem(x + d, NX)], xr.at[block], x_send.at[d], x_recv.at[d], (at_x(d), t))

    def u2_copy(d, block):
        return remote(u2.at[block], u2.at[block], u2_send.at[d], u2_recv.at[d], (at_x(d), t))

    def p_copy(d, block):
        return remote(pp.at[lax.rem(x + d, NX)], pr.at[block], p_send.at[d], p_recv.at[d], (at_x(d), t))

    def t_copy(d, block):
        return remote(pt.at[block], pt.at[block], t_send.at[d], t_recv.at[d], (f, at_t(d)))

    for d in range(1, NX):
        x_copy(d, x).start()
    for d in range(1, nq):
        d_copy(d, q).start()
    for d in range(1, nq):
        u1_copy(d, q).start()

    for name in ("q", "k", "len"):
        loads[name].wait()
    queries = jnp.concatenate(
        [
            q_v[s, :, h * HEAD : (h + 1) * HEAD].astype(F32)
            for s in range(STEPS)
            for h in range(GROUP)
        ],
        axis=0,
    ).astype(BF16)
    qb[...] = queries
    scale = HEAD**-0.5
    row = iota((ROWS, HEAD), 0)
    length = jnp.zeros((ROWS, HEAD), jnp.int32)
    for b in range(ROWS):
        length = jnp.where(row == b, len_s[b], length)
    column = iota((ROWS, SLOTS), 1)
    valid = (column // CACHE == iota((ROWS, SLOTS), 0)) & (
        lax.rem(column, CACHE) < jnp.concatenate([length] * (SLOTS // HEAD), axis=1)
    )
    scores = dot_t(queries, k_v[...].reshape(SLOTS, HEAD)) * scale
    scores = jnp.where(
        valid[None], scores.reshape(STEPS * GROUP, ROWS, SLOTS), MASKED
    ).reshape(M, SLOTS)
    peak = jnp.max(scores, axis=-1, keepdims=True)
    raised = jnp.exp(scores - peak)
    peak_c[...] = jnp.broadcast_to(peak, (M, HEAD))
    total_c[...] = jnp.broadcast_to(jnp.sum(raised, axis=-1, keepdims=True), (M, HEAD))
    loads["v"].wait()
    acc_c[...] = dot(raised.astype(BF16), v_v[...].reshape(SLOTS, HEAD))

    for d in range(1, NX):
        x_copy(d, from_x(d)).wait_recv()
    for d in range(1, nq):
        d_copy(d, from_q(d)).wait_recv()
    mine = jnp.concatenate([stack_steps(xr.at[j], slice(None)) for j in range(NX)], axis=0)
    partial = dot(mine.astype(BF16), d_all[...].reshape(nq * d_rows, HEAD))
    for j in range(NX):
        for s in range(STEPS):
            base = j * N + s * ROWS
            pp[j, s] = partial[base : base + ROWS]
    for d in range(1, NX):
        p_copy(d, x).start()
    pr[x] = pp[x]
    for d in range(1, nq):
        u1_copy(d, from_q(d)).wait_recv()
    u2[x] = u1[...].reshape(nq, 2 * HEAD).astype(BF16)
    for d in range(1, NX):
        u2_copy(d, x).start()

    for s in range(STEPS):
        xb[pl.ds(s * ROWS, ROWS)] = x_v[s].astype(F32)
    proj[...] = jnp.zeros_like(proj)

    def project(i, carry):
        w_load(i).wait()
        rows = pl.ds(pl.multiple_of(i * part, part), part)
        proj[...] += dot(
            xb[:, rows].astype(BF16), jnp.concatenate([w_v[0, rows], w_v[1, rows]], axis=1)
        )
        return carry

    lax.fori_loop(0, W_PARTS // 2, project, 0)

    loads["bias"].wait()
    half = HEAD // 2
    lane = iota((ROWS, HEAD), 1)
    frequency = jnp.exp(lax.rem(lane, half).astype(F32) * (-2.0 / HEAD * math.log(ROPE_BASE)))
    for s in range(STEPS):
        angle = (length + s).astype(F32) * frequency
        cos_v[pl.ds(s * ROWS, ROWS)] = jnp.cos(angle)
        sine = jnp.sin(angle)
        sin_v[pl.ds(s * ROWS, ROWS)] = jnp.where(lane < half, -sine, sine)

    for d in range(1, NX):
        p_copy(d, from_x(d)).wait_recv()
    for s in range(STEPS):
        pt[t, s] = pr[0, s] + pr[1, s] + pr[2, s] + pr[3, s]
    for d in range(1, ntp):
        t_copy(d, t).start()

    lax.fori_loop(W_PARTS // 2, W_PARTS, project, 0)
    bias = jnp.concatenate([bias_v[0:1], bias_v[1:2]], axis=1).astype(F32)
    proj[...] += bias
    for d in range(1, NX):
        u2_copy(d, from_x(d)).wait_recv()
    ranks = nq * NX
    order = iota((ranks, ranks), 0)
    order = iota((ranks, ranks), 1) == lax.rem(order, NX) * nq + order // NX
    up = dot(jnp.where(order, 1.0, 0.0).astype(BF16), u2[...].reshape(ranks, 2 * HEAD))
    up = up * ADAPTER_SCALE
    which = iota((ranks, 2 * HEAD), 1) < HEAD
    ublk[...] = jnp.concatenate(
        [jnp.where(which, up, 0.0), jnp.where(which, 0.0, up)], axis=0
    ).astype(BF16)

    for d in range(1, ntp):
        t_copy(d, from_t(d)).wait_recv()
    sums = []
    for s in range(STEPS):
        total = pt[0, s]
        for i in range(1, ntp):
            total = total + pt[i, s]
        sums.append(total)
    low_rank = jnp.concatenate(sums, axis=0)
    high = low_rank.astype(BF16).astype(F32)
    both = jnp.concatenate([high, low_rank - high], axis=0).astype(BF16)
    change = dot(both, ublk[...])
    fresh = proj[...] + change[:N] + change[N:]
    key = fresh[:, :HEAD]
    key = key * cos_v[...] + pltpu.roll(key, half, axis=1) * sin_v[...]
    value = fresh[:, HEAD:]
    for s in range(STEPS):
        ent_v[0, s] = key[s * ROWS : (s + 1) * ROWS].astype(BF16)
        ent_v[1, s] = value[s * ROWS : (s + 1) * ROWS].astype(BF16)
    ent_out = pltpu.make_async_copy(ent_v, ent_hbm, out_sem.at[0])
    ent_out.start()
    scores = dot_t(qb[...], key.astype(BF16)) * scale
    r, c = iota((M, N), 0), iota((M, N), 1)
    scores = jnp.where(
        (lax.rem(r, ROWS) == lax.rem(c, ROWS)) & (c // ROWS <= r // (GROUP * ROWS)), scores, MASKED
    )
    peak_old = peak_c[:, 0:1]
    peak = jnp.maximum(peak_old, jnp.max(scores, axis=-1, keepdims=True))
    raised = jnp.exp(scores - peak)
    shrink = jnp.exp(peak_old - peak)
    total = shrink * total_c[:, 0:1] + jnp.sum(raised, axis=-1, keepdims=True)
    out = (shrink * acc_c[...] + dot(raised.astype(BF16), value.astype(BF16))) / total
    for s in range(STEPS):
        for h in range(GROUP):
            base = (s * GROUP + h) * ROWS
            att_v[s, :, h * HEAD : (h + 1) * HEAD] = out[base : base + ROWS].astype(BF16)
    att_out = pltpu.make_async_copy(att_v, att_hbm, out_sem.at[1])
    att_out.start()

    for d in range(1, NX):
        x_copy(d, x).wait_send()
        p_copy(d, x).wait_send()
        u2_copy(d, x).wait_send()
    for d in range(1, nq):
        d_copy(d, q).wait_send()
        u1_copy(d, q).wait_send()
    for d in range(1, ntp):
        t_copy(d, t).wait_send()
    ent_out.wait()
    att_out.wait()


def body(ntp, x, lengths, queries, keys, values, weight, bias, down, up):
    width = x.shape[2]
    d_rows = down.shape[0]
    nq = width // (ntp * d_rows) // NX
    vmem = pltpu.VMEM
    dma = pltpu.SemaphoreType.DMA
    return pl.pallas_call(
        functools.partial(kernel, nq, ntp),
        out_shape=(
            jax.ShapeDtypeStruct(queries.shape, BF16),
            jax.ShapeDtypeStruct((2, STEPS, ROWS, HEAD), BF16),
        ),
        in_specs=[pl.BlockSpec(memory_space=pl.ANY)] * 9,
        out_specs=(pl.BlockSpec(memory_space=pl.ANY),) * 2,
        scratch_shapes=[
            vmem(x.shape, BF16),
            pltpu.SMEM(lengths.shape, jnp.int32),
            vmem(queries.shape, BF16),
            vmem(keys.shape, BF16),
            vmem(values.shape, BF16),
            vmem(weight.shape, BF16),
            vmem(bias.shape, BF16),
            vmem(up.shape, BF16),
            vmem((nq, d_rows, HEAD), BF16),
            vmem((NX, STEPS, ROWS, nq * d_rows), BF16),
            vmem((NX, STEPS, ROWS, nq * d_rows), BF16),
            vmem((nq, 1, 2 * HEAD), F32),
            vmem((NX, nq, 2 * HEAD), BF16),
            vmem((NX, STEPS, ROWS, HEAD), F32),
            vmem((NX, STEPS, ROWS, HEAD), F32),
            vmem((ntp, STEPS, ROWS, HEAD), F32),
            vmem((N, width), F32),
            vmem((N, 2 * HEAD), F32),
            vmem((N, HEAD), F32),
            vmem((N, HEAD), F32),
            vmem((M, HEAD), BF16),
            vmem((M, HEAD), F32),
            vmem((M, HEAD), F32),
            vmem((M, HEAD), F32),
            vmem((2 * nq * NX, 2 * HEAD), BF16),
            vmem(queries.shape, BF16),
            vmem((2, STEPS, ROWS, HEAD), BF16),
            dma((8,)),
            dma((W_PARTS,)),
            dma((2,)),
            dma((nq,)),
            dma((nq,)),
            dma((NX,)),
            dma((NX,)),
            dma((nq,)),
            dma((nq,)),
            dma((NX,)),
            dma((NX,)),
            dma((NX,)),
            dma((NX,)),
            dma((ntp,)),
            dma((ntp,)),
        ],
        compiler_params=pltpu.CompilerParams(
            collective_id=0, has_side_effects=True, vmem_limit_bytes=48 * 1024 * 1024
        ),
        name="adapter_attention",
    )(x, lengths, queries, keys, values, weight, bias, down, up)


def solution(mesh):
    placed = (
        P(None, "fsdp", None),
        P("fsdp"),
        P(None, "fsdp", "tp"),
        P("fsdp", None, "tp"),
        P("fsdp", None, "tp"),
        P(None, None, "tp"),
        P(None, "tp"),
        P(("fsdp", "tp"), None),
        P(None, "fsdp", "tp"),
    )
    return jax.shard_map(
        functools.partial(body, mesh.shape["tp"]),
        mesh=mesh,
        in_specs=placed,
        out_specs=(P(None, "fsdp", "tp"), P(None, None, "fsdp", "tp")),
        check_vma=False,
    )
```

time: 790 us -> 42.8 us (0.05)
  waiting for transfers between devices: 566 us -> 0 us
  blocking collectives: 199 us -> 0 us
  Pallas kernels: 0 us -> 32.1 us
  between operations: 14.1 us -> 0.65 us
    all_gather x1 -> x0, waiting for transfers between devices: 565 us -> none  [body(): lax.all_gather(adapter_down_weight, ('fsdp', 'tp'), axis=0, tiled=True)]
    all_gather x1 -> x0, blocking collectives: 199 us -> none  [body(): lax.all_gather(adapter_up_weight, 'fsdp', axis=1, tiled=True)]
    pallas_call x0 -> x1, Pallas kernels: none -> 32.1 us  [body(): pl.pallas_call(functools.partial(kernel, nq, ntp), out_shape=(jax.ShapeDt...]
  transfers between devices with their start and end apart: 1 -> 0, of which waited for: 1 -> 0; matrix products, arithmetic and copies ran while one was open for 0% -> 0% of each run, Pallas kernels for 0% -> 0%
where the time goes in v1:
time: 42.8 us; the launch traced here: 42.4 us
  Pallas kernels  32.1 us (75%)
  local copies, waits for them, and re-layouts  9.66 us (23%)
  between operations  0.65 us (2%)
    pallas_call x1, Pallas kernels, body(): pl.pallas_call(functools.partial(kernel, nq, ntp), out_shape=(jax.ShapeDt...  32.1 us
    unnamed x19, local copies, waits for them, and re-layouts  9.66 us

profile of v1, /device:TPU:1, one launch (start us, length us, event | category | flops | bytes accessed | tf_op | source)
XLA Modules:
  0.0 42.4 jit_solution(17977588597982285067)
XLA Ops:
  0.6 0.7 %copy.11.u_hbm = bf16[2,1,128]{2,1,0:T(2,128)(2,1)S(1)} copy(bf16[2,1,128]{2,0,1:T(2,128)(2,1)} %param.17) | data formatting | bytes 1024 | tf_op args[8]
  1.3 0.0 copy-start
  1.3 2.2 %copy-done = bf16[2,8192,128]{2,1,0:T(8,128)(2,1)S(1)} copy-done((bf16[2,8192,128]{2,1,0:T(8,128)(2,1)S(1)}, bf16[2,8192,128]{2,1,0:T(8,128)(2,1)}, u32[]{:S(2)}) %copy-start) | copy-done | bytes 4194328
  3.5 0.0 copy-start.1
  3.5 1.0 %copy-done.1 = bf16[3,8,8192]{2,1,0:T(8,128)(2,1)S(1)} copy-done((bf16[3,8,8192]{2,1,0:T(8,128)(2,1)S(1)}, bf16[3,8,8192]{2,1,0:T(8,128)(2,1)}, u32[]{:S(2)}) %copy-start.1) | copy-done | bytes 393240
  4.5 0.0 copy-start.2
  4.5 0.9 %copy-done.2 = bf16[8,64,128]{2,1,0:T(8,128)(2,1)S(1)} copy-done((bf16[8,64,128]{2,1,0:T(8,128)(2,1)S(1)}, bf16[8,64,128]{2,1,0:T(8,128)(2,1)}, u32[]{:S(2)}) %copy-start.2) | copy-done | bytes 131096
  5.4 0.0 copy-start.3
  5.4 0.9 %copy-done.3 = bf16[8,64,128]{2,1,0:T(8,128)(2,1)S(1)} copy-done((bf16[8,64,128]{2,1,0:T(8,128)(2,1)S(1)}, bf16[8,64,128]{2,1,0:T(8,128)(2,1)}, u32[]{:S(2)}) %copy-start.3) | copy-done | bytes 131096
  6.3 0.0 copy-start.4
  6.3 0.8 %copy-done.4 = bf16[3,8,1024]{2,1,0:T(8,128)(2,1)S(1)} copy-done((bf16[3,8,1024]{2,1,0:T(8,128)(2,1)S(1)}, bf16[3,8,1024]{2,1,0:T(8,128)(2,1)}, u32[]{:S(2)}) %copy-start.4) | copy-done | bytes 49176
  7.1 0.0 copy-start.5
  7.1 0.7 %copy-done.5 = bf16[16,128]{1,0:T(8,128)(2,1)S(1)} copy-done((bf16[16,128]{1,0:T(8,128)(2,1)S(1)}, bf16[16,128]{1,0:T(8,128)(2,1)}, u32[]{:S(2)}) %copy-start.5) | copy-done | bytes 4120
  7.8 0.0 copy-start.6
  7.8 0.7 %copy-done.6 = s32[8]{0:T(128)S(1)} copy-done((s32[8]{0:T(128)S(1)}, s32[8]{0:T(128)}, u32[]{:S(2)}) %copy-start.6) | copy-done | bytes 56
  8.4 0.0 copy-start.7
  8.4 0.7 %copy-done.7 = bf16[2,128]{1,0:T(2,128)(2,1)S(1)} copy-done((bf16[2,128]{1,0:T(2,128)(2,1)S(1)}, bf16[2,128]{1,0:T(2,128)(2,1)}, u32[]{:S(2)}) %copy-start.7) | copy-done | bytes 536
  9.1 32.1 %adapter_attention.1 = (bf16[3,8,1024]{2,1,0:T(8,128)(2,1)S(1)}, bf16[2,3,8,128]{3,2,1,0:T(8,128)(2,1)S(1)}) custom-call(bf16[3,8,8192]{2,1,0:T(8,128)(2,1)S(1)} %copy-done.1, s32[8]{0:T(128)S(1)} %copy-done.6, bf16[3,8,1024]{2,1,0:T(8,128)(2,1)S(1)} %copy-done.4, bf16[8,64,128]{2,1,0:T(8,128)(2,1)S(1)} %copy-done.2, bf16[8,64,128]{2,1,0:T(8,128)(2,1)S(1)} %copy-done.3, ...), custom_call_target="tpu_custom_call" | custom-call | tf_op jit(solution)/shard_map/adapter_attention/pallas_call | solution.py:379
  41.2 0.6 %copy.14 = bf16[3,8,1024]{2,1,0:T(8,128)(2,1)} copy(bf16[3,8,1024]{2,1,0:T(8,128)(2,1)S(1)} %get-tuple-element.4) | data formatting | bytes 98304
  41.8 0.6 %copy.15 = bf16[2,3,8,128]{3,2,1,0:T(8,128)(2,1)} copy(bf16[2,3,8,128]{3,2,1,0:T(8,128)(2,1)S(1)} %get-tuple-element.5) | data formatting | bytes 24576
Async XLA Ops:
  1.3 2.2 %copy-start = (bf16[2,8192,128]{2,1,0:T(8,128)(2,1)S(1)}, bf16[2,8192,128]{2,1,0:T(8,128)(2,1)}, u32[]{:S(2)}) copy-start(bf16[2,8192,128]{2,1,0:T(8,128)(2,1)} %w_hbm.1) | copy-start | bytes 12582916
  3.5 1.0 %copy-start.1 = (bf16[3,8,8192]{2,1,0:T(8,128)(2,1)S(1)}, bf16[3,8,8192]{2,1,0:T(8,128)(2,1)}, u32[]{:S(2)}) copy-start(bf16[3,8,8192]{2,1,0:T(8,128)(2,1)} %x_hbm.1) | copy-start | bytes 1179652
  4.5 0.9 %copy-start.2 = (bf16[8,64,128]{2,1,0:T(8,128)(2,1)S(1)}, bf16[8,64,128]{2,1,0:T(8,128)(2,1)}, u32[]{:S(2)}) copy-start(bf16[8,64,128]{2,1,0:T(8,128)(2,1)} %k_hbm.1) | copy-start | bytes 393220
  5.4 0.9 %copy-start.3 = (bf16[8,64,128]{2,1,0:T(8,128)(2,1)S(1)}, bf16[8,64,128]{2,1,0:T(8,128)(2,1)}, u32[]{:S(2)}) copy-start(bf16[8,64,128]{2,1,0:T(8,128)(2,1)} %v_hbm.1) | copy-start | bytes 393220
  6.3 0.8 %copy-start.4 = (bf16[3,8,1024]{2,1,0:T(8,128)(2,1)S(1)}, bf16[3,8,1024]{2,1,0:T(8,128)(2,1)}, u32[]{:S(2)}) copy-start(bf16[3,8,1024]{2,1,0:T(8,128)(2,1)} %q_hbm.1) | copy-start | bytes 147460
  7.1 0.7 %copy-start.5 = (bf16[16,128]{1,0:T(8,128)(2,1)S(1)}, bf16[16,128]{1,0:T(8,128)(2,1)}, u32[]{:S(2)}) copy-start(bf16[16,128]{1,0:T(8,128)(2,1)} %d_hbm.1) | copy-start | bytes 12292
  7.8 0.7 %copy-start.6 = (s32[8]{0:T(128)S(1)}, s32[8]{0:T(128)}, u32[]{:S(2)}) copy-start(s32[8]{0:T(128)} %len_hbm.1) | copy-start | bytes 100
  8.4 0.7 %copy-start.7 = (bf16[2,128]{1,0:T(2,128)(2,1)S(1)}, bf16[2,128]{1,0:T(2,128)(2,1)}, u32[]{:S(2)}) copy-start(bf16[2,128]{1,0:T(2,128)(2,1)} %bias_hbm.1) | copy-start | bytes 1540

commit v2 on v1

--- a/solution.py
+++ b/solution.py
@@ -54,8 +54,8 @@
     bias_hbm,
     d_hbm,
     u_hbm,
-    att_hbm,
-    ent_hbm,
+    att_v,
+    ent_v,
     x_v,
     len_s,
     q_v,
@@ -81,11 +81,8 @@
     total_c,
     acc_c,
     ublk,
-    att_v,
-    ent_v,
     in_sem,
     w_sem,
-    out_sem,
     d_send,
     d_recv,
     x_send,
@@ -148,7 +145,7 @@
         pl.semaphore_signal(barrier, inc=1, device_id=(f, at_t(d)), device_id_type=MESH)
 
     loads["u"].wait()
-    u1[q] = jnp.concatenate([u_v[0], u_v[1]], axis=1).astype(F32)
+    u1[q] = jnp.concatenate([u_v[0:1].astype(F32), u_v[1:2].astype(F32)], axis=1)
     span = ntp * d_rows
     per = HEAD // d_rows
     groups = nq // per
@@ -337,8 +334,6 @@
     for s in range(STEPS):
         ent_v[0, s] = key[s * ROWS : (s + 1) * ROWS].astype(BF16)
         ent_v[1, s] = value[s * ROWS : (s + 1) * ROWS].astype(BF16)
-    ent_out = pltpu.make_async_copy(ent_v, ent_hbm, out_sem.at[0])
-    ent_out.start()
     scores = dot_t(qb[...], key.astype(BF16)) * scale
     r, c = iota((M, N), 0), iota((M, N), 1)
     scores = jnp.where(
@@ -354,8 +349,6 @@
         for h in range(GROUP):
             base = (s * GROUP + h) * ROWS
             att_v[s, :, h * HEAD : (h + 1) * HEAD] = out[base : base + ROWS].astype(BF16)
-    att_out = pltpu.make_async_copy(att_v, att_hbm, out_sem.at[1])
-    att_out.start()
 
     for d in range(1, NX):
         x_copy(d, x).wait_send()
@@ -366,8 +359,17 @@
         u1_copy(d, q).wait_send()
     for d in range(1, ntp):
         t_copy(d, t).wait_send()
-    ent_out.wait()
-    att_out.wait()
+
+
+def deliver(att_v, ent_v, att_hbm, ent_hbm, sem):
+    copies = [
+        pltpu.make_async_copy(att_v, att_hbm, sem.at[0]),
+        pltpu.make_async_copy(ent_v, ent_hbm, sem.at[1]),
+    ]
+    for copy in copies:
+        copy.start()
+    for copy in copies:
+        copy.wait()
 
 
 def body(ntp, x, lengths, queries, keys, values, weight, bias, down, up):
@@ -376,14 +378,14 @@
     nq = width // (ntp * d_rows) // NX
     vmem = pltpu.VMEM
     dma = pltpu.SemaphoreType.DMA
-    return pl.pallas_call(
+    anywhere = pl.BlockSpec(memory_space=pl.ANY)
+    inside = pl.BlockSpec(memory_space=pltpu.VMEM)
+    entries = (2, STEPS, ROWS, HEAD)
+    attended, entry = pl.pallas_call(
         functools.partial(kernel, nq, ntp),
-        out_shape=(
-            jax.ShapeDtypeStruct(queries.shape, BF16),
-            jax.ShapeDtypeStruct((2, STEPS, ROWS, HEAD), BF16),
-        ),
-        in_specs=[pl.BlockSpec(memory_space=pl.ANY)] * 9,
-        out_specs=(pl.BlockSpec(memory_space=pl.ANY),) * 2,
+        out_shape=(pltpu.VMEM(queries.shape, BF16), pltpu.VMEM(entries, BF16)),
+        in_specs=[anywhere] * 9,
+        out_specs=(inside, inside),
         scratch_shapes=[
             vmem(x.shape, BF16),
             pltpu.SMEM(lengths.shape, jnp.int32),
@@ -392,7 +394,7 @@
             vmem(values.shape, BF16),
             vmem(weight.shape, BF16),
             vmem(bias.shape, BF16),
-            vmem(up.shape, BF16),
+            vmem((2, HEAD), BF16),
             vmem((nq, d_rows, HEAD), BF16),
             vmem((NX, STEPS, ROWS, nq * d_rows), BF16),
             vmem((NX, STEPS, ROWS, nq * d_rows), BF16),
@@ -410,11 +412,8 @@
             vmem((M, HEAD), F32),
             vmem((M, HEAD), F32),
             vmem((2 * nq * NX, 2 * HEAD), BF16),
-            vmem(queries.shape, BF16),
-            vmem((2, STEPS, ROWS, HEAD), BF16),
             dma((8,)),
             dma((W_PARTS,)),
-            dma((2,)),
             dma((nq,)),
             dma((nq,)),
             dma((NX,)),
@@ -429,10 +428,22 @@
             dma((ntp,)),
         ],
         compiler_params=pltpu.CompilerParams(
-            collective_id=0, has_side_effects=True, vmem_limit_bytes=48 * 1024 * 1024
+            collective_id=0, has_side_effects=True, vmem_limit_bytes=60 * 1024 * 1024
         ),
         name="adapter_attention",
-    )(x, lengths, queries, keys, values, weight, bias, down, up)
+    )(x, lengths, queries, keys, values, weight, bias, down, up.reshape(2, HEAD))
+    return pl.pallas_call(
+        deliver,
+        out_shape=(
+            jax.ShapeDtypeStruct(queries.shape, BF16),
+            jax.ShapeDtypeStruct(entries, BF16),
+        ),
+        in_specs=[inside] * 2,
+        out_specs=(anywhere, anywhere),
+        scratch_shapes=[dma((2,))],
+        compiler_params=pltpu.CompilerParams(vmem_limit_bytes=1024 * 1024),
+        name="deliver",
+    )(attended, entry)
 
 
 def solution(mesh):

time: 42.8 us -> 32.9 us (0.77)
  local copies, waits for them, and re-layouts: 9.66 us -> 0 us
    unnamed x19 -> x0, local copies, waits for them, and re-layouts: 9.66 us -> none
    pallas_call x1 -> x2, Pallas kernels: 32.1 us -> 32.1 us  [the longest x1 31.5 us: body(): pl.pallas_call(functools.partial(kernel, nq, ntp), out_shape=(pltpu.VMEM(...]
where the time goes in v2:
time: 32.9 us; the launch traced here: 32.8 us
  Pallas kernels  32.1 us (98%)
  between operations  0.64 us (2%)
    pallas_call x1, Pallas kernels, body(): pl.pallas_call(functools.partial(kernel, nq, ntp), out_shape=(pltpu.VMEM(...  31.5 us

profile of v2, /device:TPU:1, one launch (start us, length us, event | category | flops | bytes accessed | tf_op | source)
XLA Modules:
  0.0 32.8 jit_solution(10200113362664456705)
XLA Ops:
  0.6 31.5 %adapter_attention.1 = (bf16[3,8,1024]{2,1,0:T(8,128)(2,1)S(1)}, bf16[2,3,8,128]{3,2,1,0:T(8,128)(2,1)S(1)}) custom-call(bf16[3,8,8192]{2,1,0:T(8,128)(2,1)} %x_hbm.1, s32[8]{0:T(128)} %len_hbm.1, bf16[3,8,1024]{2,1,0:T(8,128)(2,1)} %q_hbm.1, bf16[8,64,128]{2,1,0:T(8,128)(2,1)} %k_hbm.1, bf16[8,64,128]{2,1,0:T(8,128)(2,1)} %v_hbm.1, ...), custom_call_target="tpu_custom_call" | custom-call | tf_op jit(solution)/shard_map/adapter_attention/pallas_call | solution.py:384
  32.1 0.6 %deliver.1 = (bf16[3,8,1024]{2,1,0:T(8,128)(2,1)}, bf16[2,3,8,128]{3,2,1,0:T(8,128)(2,1)}) custom-call(bf16[3,8,1024]{2,1,0:T(8,128)(2,1)S(1)} %get-tuple-element.4.att_v, bf16[2,3,8,128]{3,2,1,0:T(8,128)(2,1)S(1)} %get-tuple-element.5.ent_v), custom_call_target="tpu_custom_call" | custom-call | tf_op jit(solution)/shard_map/deliver/pallas_call | solution.py:435

commit v3 on v2

v3 whole, which is shorter than its diff:
```python
import math

import jax
import jax.numpy as jnp
from jax import lax
from jax.experimental import pallas as pl
from jax.experimental.pallas import tpu as pltpu
from jax.sharding import PartitionSpec as P

HEAD = 128
GROUP = 8
STEPS = 3
ROWS = 8
CACHE = 64
NX = 4
NY = 8
NQ = 16
NT = 8
D_ROWS = 16
ADAPTER_SCALE = 2.0
ROPE_BASE = 1000000.0
MASKED = -1e30
MESH = pl.DeviceIdType.MESH
F32 = jnp.float32
BF16 = jnp.bfloat16
N = STEPS * ROWS
M = STEPS * GROUP * ROWS
SLOTS = ROWS * CACHE
W_PARTS = 8
Y_ORDER = (0, 1, 2, 3, 7, 6, 5, 4)


def iota(shape, dim):
    return lax.broadcasted_iota(jnp.int32, shape, dim)


def dot(a, b):
    return jnp.dot(a, b, preferred_element_type=F32)


def dot_t(a, b):
    return lax.dot_general(a, b, (((1,), (1,)), ((), ())), preferred_element_type=F32)


def stack_steps(ref, columns):
    return jnp.concatenate([ref[s, :, columns].astype(F32) for s in range(STEPS)], axis=0)


def kernel(
    x_hbm,
    len_hbm,
    q_hbm,
    k_hbm,
    v_hbm,
    w_hbm,
    bias_hbm,
    d_hbm,
    u_hbm,
    att_v,
    ent_v,
    x_v,
    len_s,
    q_v,
    k_v,
    v_v,
    w_v,
    bias_v,
    u_v,
    u_own,
    d_all,
    xs,
    xr,
    u1,
    u2,
    pp,
    pr,
    pt,
    xb,
    proj,
    cos_v,
    sin_v,
    qb,
    peak_c,
    total_c,
    acc_c,
    ublk,
    in_sem,
    w_sem,
    d_send,
    d_recv,
    df_sem,
    x_send,
    x_recv,
    u1_send,
    u1_recv,
    uf_sem,
    u2_send,
    u2_recv,
    p_send,
    p_recv,
    t_send,
    t_recv,
    near_in,
    go,
):
    f = lax.axis_index("fsdp")
    t = lax.axis_index("tp")
    q, x = f // NX, lax.rem(f, NX)
    y, half = q // 2, lax.rem(q, 2)
    mirror = (NT // 2 - 1 - t // 2) * 2 + lax.rem(t, 2)
    width = x_v.shape[2]

    def at(yy, hh, xx):
        return (yy * 2 + hh) * NX + xx

    def plus(i, d, n):
        return lax.rem(i + d, n)

    def load(i, src, dst):
        copy = pltpu.make_async_copy(src, dst, in_sem.at[i])
        copy.start()
        return copy

    loads = {
        "u": load(0, u_hbm, u_v),
        "x": load(1, x_hbm, x_v),
        "len": load(2, len_hbm, len_s),
        "bias": load(3, bias_hbm, bias_v),
        "q": load(4, q_hbm, q_v),
        "k": load(5, k_hbm, k_v),
        "v": load(6, v_hbm, v_v),
    }
    d_load = pltpu.make_async_copy(d_hbm, d_all.at[q], in_sem.at[7])
    part = width // W_PARTS

    def w_load(i):
        rows = pl.ds(pl.multiple_of(i * part, part), part)
        return pltpu.make_async_copy(w_hbm.at[:, rows], w_v.at[:, rows], w_sem.at[i])

    def remote(src, dst, send, recv, where):
        return pltpu.make_async_remote_copy(
            src_ref=src, dst_ref=dst, send_sem=send, recv_sem=recv, device_id=where, device_id_type=MESH
        )

    def d_out(yy):
        where = (at(yy, 0, x), jnp.where(half == 0, t, mirror))
        return remote(d_hbm, d_all.at[q], d_send.at[yy], d_recv.at[q], where)

    def d_in(qq):
        return remote(d_hbm, d_all.at[qq], d_send.at[0], d_recv.at[qq], (f, t))

    def u1_out(yy):
        return remote(u_own, u1.at[q], u1_send.at[yy], u1_recv.at[q], (at(yy, 0, x), t))

    def u1_in(qq):
        return remote(u_own, u1.at[qq], u1_send.at[0], u1_recv.at[qq], (f, t))

    def d_over():
        return remote(d_all, d_all, df_sem.at[0], df_sem.at[1], (at(y, 1 - half, x), mirror))

    def u1_over():
        return remote(u1, u1, uf_sem.at[0], uf_sem.at[1], (at(y, 1 - half, x), t))

    def along_x(src, dst, send, recv, d):
        return remote(src, dst, send.at[d], recv.at[d], (at(y, half, plus(x, d, NX)), t))

    def x_copy(d, block):
        return along_x(xs.at[plus(x, d, NX)], xr.at[block], x_send, x_recv, d)

    def p_copy(d, block):
        return along_x(pp.at[plus(x, d, NX)], pr.at[block], p_send, p_recv, d)

    def u2_copy(d, block):
        return along_x(u2.at[block], u2.at[block], u2_send, u2_recv, d)

    def t_copy(d, block):
        return remote(pt.at[block], pt.at[block], t_send.at[d], t_recv.at[d], (f, plus(t, d, NT)))

    def from_x(d):
        return plus(x, NX - d, NX)

    def from_t(d):
        return plus(t, NT - d, NT)

    barrier = pltpu.get_barrier_semaphore()

    def signal(semaphore, where):
        pl.semaphore_signal(semaphore, inc=1, device_id=where, device_id_type=MESH)

    @pl.when(half == 0)
    def _():
        d_load.start()
        for yy in Y_ORDER:
            signal(barrier, (at(yy, 1, x), mirror))
            signal(barrier, (at(yy, 1, x), t))
        for d in range(1, NY):
            signal(barrier, (at(plus(y, d, NY), 0, x), t))
        for d in range(1, NX):
            signal(barrier, (at(y, 0, plus(x, d, NX)), t))
        for d in range(1, NT):
            signal(barrier, (f, plus(t, d, NT)))

    pl.semaphore_wait(barrier, jnp.where(half == 0, NY + NX + NT - 3, 2 * NY))

    @pl.when(half == 1)
    def _():
        for yy in Y_ORDER:
            d_out(yy).start()

    @pl.when(half == 0)
    def _():
        for d in range(1, NY):
            d_out(plus(y, d, NY)).start()

    loads["u"].wait()
    u_own[...] = jnp.concatenate([u_v[0:1].astype(F32), u_v[1:2].astype(F32)], axis=1)

    @pl.when(half == 1)
    def _():
        for yy in Y_ORDER:
            u1_out(yy).start()

    @pl.when(half == 0)
    def _():
        u1[q] = u_own[...]
        for d in range(1, NY):
            u1_out(plus(y, d, NY)).start()

    for i in range(W_PARTS):
        w_load(i).start()

    span = NT * D_ROWS
    per = HEAD // D_ROWS
    groups = NQ // per
    shape = (per * span, HEAD)
    block = iota(shape, 1) // D_ROWS
    owner = jnp.where(lax.rem(block, 2) == half, t, mirror)
    pick = (iota(shape, 0) // span == block) & (
        lax.rem(iota(shape, 0), span) == owner * D_ROWS + lax.rem(iota(shape, 1), D_ROWS)
    )
    pick = jnp.where(pick, 1.0, 0.0).astype(BF16)
    loads["x"].wait()
    rows = []
    for j in range(NX):
        for g in range(groups):
            rows.append(
                jnp.concatenate(
                    [
                        stack_steps(x_v, pl.ds(((g * per + i) * NX + j) * span, span))
                        for i in range(per)
                    ],
                    axis=1,
                )
            )
    picked = dot(jnp.concatenate(rows, axis=0).astype(BF16), pick)
    for j in range(NX):
        for g in range(groups):
            base = (j * groups + g) * N
            for s in range(STEPS):
                xs[j, s, :, g * HEAD : (g + 1) * HEAD] = picked[
                    base + s * ROWS : base + (s + 1) * ROWS
                ].astype(BF16)
    xr[x] = xs[x]
    @pl.when(half == 0)
    def _():
        for d in range(1, NX):
            x_copy(d, x).start()

    for name in ("q", "k", "len"):
        loads[name].wait()
    queries = jnp.concatenate(
        [
            q_v[s, :, h * HEAD : (h + 1) * HEAD].astype(F32)
            for s in range(STEPS)
            for h in range(GROUP)
        ],
        axis=0,
    ).astype(BF16)
    qb[...] = queries
    scale = HEAD**-0.5
    row = iota((ROWS, HEAD), 0)
    length = jnp.zeros((ROWS, HEAD), jnp.int32)
    for b in range(ROWS):
        length = jnp.where(row == b, len_s[b], length)
    column = iota((ROWS, SLOTS), 1)
    valid = (column // CACHE == iota((ROWS, SLOTS), 0)) & (
        lax.rem(column, CACHE) < jnp.concatenate([length] * (SLOTS // HEAD), axis=1)
    )
    scores = dot_t(queries, k_v[...].reshape(SLOTS, HEAD)) * scale
    scores = jnp.where(
        valid[None], scores.reshape(STEPS * GROUP, ROWS, SLOTS), MASKED
    ).reshape(M, SLOTS)
    peak = jnp.max(scores, axis=-1, keepdims=True)
    raised = jnp.exp(scores - peak)
    peak_c[...] = jnp.broadcast_to(peak, (M, HEAD))
    total_c[...] = jnp.broadcast_to(jnp.sum(raised, axis=-1, keepdims=True), (M, HEAD))
    loads["v"].wait()
    acc_c[...] = dot(raised.astype(BF16), v_v[...].reshape(SLOTS, HEAD))

    for s in range(STEPS):
        xb[pl.ds(s * ROWS, ROWS)] = x_v[s].astype(F32)
    proj[...] = jnp.zeros_like(proj)

    def project(i, carry):
        w_load(i).wait()
        rows = pl.ds(pl.multiple_of(i * part, part), part)
        proj[...] += dot(
            xb[:, rows].astype(BF16), jnp.concatenate([w_v[0, rows], w_v[1, rows]], axis=1)
        )
        return carry

    lax.fori_loop(0, W_PARTS, project, 0)

    loads["bias"].wait()
    proj[...] += jnp.concatenate([bias_v[0:1], bias_v[1:2]], axis=1).astype(F32)
    turn = HEAD // 2
    lane = iota((ROWS, HEAD), 1)
    frequency = jnp.exp(lax.rem(lane, turn).astype(F32) * (-2.0 / HEAD * math.log(ROPE_BASE)))
    for s in range(STEPS):
        angle = (length + s).astype(F32) * frequency
        cos_v[pl.ds(s * ROWS, ROWS)] = jnp.cos(angle)
        sine = jnp.sin(angle)
        sin_v[pl.ds(s * ROWS, ROWS)] = jnp.where(lane < turn, -sine, sine)

    @pl.when(half == 0)
    def _():
        d_load.wait()
        d_in(q + 1).wait_recv()
        for d in range(1, NX):
            signal(near_in, (at(y, 0, plus(x, d, NX)), t))
        for d in range(1, NT):
            signal(near_in, (f, plus(t, d, NT)))
        pl.semaphore_wait(near_in, NX + NT - 2)
        signal(go, (at(y, 1, x), mirror))
        for d in range(1, NY):
            d_in(plus(y, d, NY) * 2).wait_recv()
            d_in(plus(y, d, NY) * 2 + 1).wait_recv()

    @pl.when(half == 1)
    def _():
        pl.semaphore_wait(go, 1)
        for d in range(1, NX):
            x_copy(d, x).start()
        d_over().wait_recv()

    for d in range(1, NX):
        x_copy(d, from_x(d)).wait_recv()
    mine = jnp.concatenate([stack_steps(xr.at[j], slice(None)) for j in range(NX)], axis=0)
    partial = dot(mine.astype(BF16), d_all[...].reshape(NQ * D_ROWS, HEAD))
    for j in range(NX):
        for s in range(STEPS):
            base = j * N + s * ROWS
            pp[j, s] = partial[base : base + ROWS]
    for d in range(1, NX):
        p_copy(d, x).start()
    pr[x] = pp[x]

    @pl.when(half == 0)
    def _():
        d_over().start()
        for d in range(1, NY):
            u1_in(plus(y, d, NY) * 2).wait_recv()
        for yy in range(NY):
            u1_in(yy * 2 + 1).wait_recv()
        u1_over().start()

    @pl.when(half == 1)
    def _():
        u1_over().wait_recv()

    u2[x] = u1[...].reshape(NQ, 2 * HEAD).astype(BF16)
    for d in range(1, NX):
        u2_copy(d, x).start()

    for d in range(1, NX):
        p_copy(d, from_x(d)).wait_recv()
    for s in range(STEPS):
        pt[t, s] = pr[0, s] + pr[1, s] + pr[2, s] + pr[3, s]
    for d in range(1, NT):
        t_copy(d, t).start()

    for d in range(1, NX):
        u2_copy(d, from_x(d)).wait_recv()
    ranks = NQ * NX
    order = iota((ranks, ranks), 0)
    order = iota((ranks, ranks), 1) == lax.rem(order, NX) * NQ + order // NX
    up = dot(jnp.where(order, 1.0, 0.0).astype(BF16), u2[...].reshape(ranks, 2 * HEAD))
    up = up * ADAPTER_SCALE
    which = iota((ranks, 2 * HEAD), 1) < HEAD
    ublk[...] = jnp.concatenate(
        [jnp.where(which, up, 0.0), jnp.where(which, 0.0, up)], axis=0
    ).astype(BF16)

    @pl.when(half == 0)
    def _():
        for d in range(1, NY):
            d_out(plus(y, d, NY)).wait_send()
            u1_out(plus(y, d, NY)).wait_send()
        d_over().wait_send()
        u1_over().wait_send()

    @pl.when(half == 1)
    def _():
        for yy in range(NY):
            d_out(yy).wait_send()
            u1_out(yy).wait_send()

    for d in range(1, NX):
        x_copy(d, x).wait_send()
        p_copy(d, x).wait_send()
        u2_copy(d, x).wait_send()

    for d in range(1, NT):
        t_copy(d, from_t(d)).wait_recv()
    sums = []
    for s in range(STEPS):
        total = pt[0, s]
        for i in range(1, NT):
            total = total + pt[i, s]
        sums.append(total)
    low_rank = jnp.concatenate(sums, axis=0)
    high = low_rank.astype(BF16).astype(F32)
    both = jnp.concatenate([high, low_rank - high], axis=0).astype(BF16)
    change = dot(both, ublk[...])
    fresh = proj[...] + change[:N] + change[N:]
    key = fresh[:, :HEAD]
    key = key * cos_v[...] + pltpu.roll(key, turn, axis=1) * sin_v[...]
    value = fresh[:, HEAD:]
    for s in range(STEPS):
        ent_v[0, s] = key[s * ROWS : (s + 1) * ROWS].astype(BF16)
        ent_v[1, s] = value[s * ROWS : (s + 1) * ROWS].astype(BF16)
    scores = dot_t(qb[...], key.astype(BF16)) * scale
    r, c = iota((M, N), 0), iota((M, N), 1)
    scores = jnp.where(
        (lax.rem(r, ROWS) == lax.rem(c, ROWS)) & (c // ROWS <= r // (GROUP * ROWS)), scores, MASKED
    )
    peak_old = peak_c[:, 0:1]
    peak = jnp.maximum(peak_old, jnp.max(scores, axis=-1, keepdims=True))
    raised = jnp.exp(scores - peak)
    shrink = jnp.exp(peak_old - peak)
    total = shrink * total_c[:, 0:1] + jnp.sum(raised, axis=-1, keepdims=True)
    out = (shrink * acc_c[...] + dot(raised.astype(BF16), value.astype(BF16))) / total
    for s in range(STEPS):
        for h in range(GROUP):
            base = (s * GROUP + h) * ROWS
            att_v[s, :, h * HEAD : (h + 1) * HEAD] = out[base : base + ROWS].astype(BF16)

    for d in range(1, NT):
        t_copy(d, t).wait_send()


def deliver(att_v, ent_v, att_hbm, ent_hbm, sem):
    copies = [
        pltpu.make_async_copy(att_v, att_hbm, sem.at[0]),
        pltpu.make_async_copy(ent_v, ent_hbm, sem.at[1]),
    ]
    for copy in copies:
        copy.start()
    for copy in copies:
        copy.wait()


def body(x, lengths, queries, keys, values, weight, bias, down, up):
    width = x.shape[2]
    vmem = pltpu.VMEM
    dma = pltpu.SemaphoreType.DMA
    anywhere = pl.BlockSpec(memory_space=pl.ANY)
    inside = pl.BlockSpec(memory_space=pltpu.VMEM)
    entries = (2, STEPS, ROWS, HEAD)
    attended, entry = pl.pallas_call(
        kernel,
        out_shape=(pltpu.VMEM(queries.shape, BF16), pltpu.VMEM(entries, BF16)),
        in_specs=[anywhere] * 9,
        out_specs=(inside, inside),
        scratch_shapes=[
            vmem(x.shape, BF16),
            pltpu.SMEM(lengths.shape, jnp.int32),
            vmem(queries.shape, BF16),
            vmem(keys.shape, BF16),
            vmem(values.shape, BF16),
            vmem(weight.shape, BF16),
            vmem(bias.shape, BF16),
            vmem((2, HEAD), BF16),
            vmem((1, 2 * HEAD), F32),
            vmem((NQ, D_ROWS, HEAD), BF16),
            vmem((NX, STEPS, ROWS, NQ * D_ROWS), BF16),
            vmem((NX, STEPS, ROWS, NQ * D_ROWS), BF16),
            vmem((NQ, 1, 2 * HEAD), F32),
            vmem((NX, NQ, 2 * HEAD), BF16),
            vmem((NX, STEPS, ROWS, HEAD), F32),
            vmem((NX, STEPS, ROWS, HEAD), F32),
            vmem((NT, STEPS, ROWS, HEAD), F32),
            vmem((N, width), F32),
            vmem((N, 2 * HEAD), F32),
            vmem((N, HEAD), F32),
            vmem((N, HEAD), F32),
            vmem((M, HEAD), BF16),
            vmem((M, HEAD), F32),
            vmem((M, HEAD), F32),
            vmem((M, HEAD), F32),
            vmem((2 * NQ * NX, 2 * HEAD), BF16),
            dma((8,)),
            dma((W_PARTS,)),
            dma((NY,)),
            dma((NQ,)),
            dma((2,)),
            dma((NX,)),
            dma((NX,)),
            dma((NY,)),
            dma((NQ,)),
            dma((2,)),
            dma((NX,)),
            dma((NX,)),
            dma((NX,)),
            dma((NX,)),
            dma((NT,)),
            dma((NT,)),
            pltpu.SemaphoreType.REGULAR,
            pltpu.SemaphoreType.REGULAR,
        ],
        compiler_params=pltpu.CompilerParams(
            collective_id=0, has_side_effects=True, vmem_limit_bytes=60 * 1024 * 1024
        ),
        name="adapter_attention",
    )(x, lengths, queries, keys, values, weight, bias, down, up.reshape(2, HEAD))
    return pl.pallas_call(
        deliver,
        out_shape=(
            jax.ShapeDtypeStruct(queries.shape, BF16),
            jax.ShapeDtypeStruct(entries, BF16),
        ),
        in_specs=[inside] * 2,
        out_specs=(anywhere, anywhere),
        scratch_shapes=[dma((2,))],
        compiler_params=pltpu.CompilerParams(vmem_limit_bytes=1024 * 1024),
        name="deliver",
    )(attended, entry)


def solution(mesh):
    placed = (
        P(None, "fsdp", None),
        P("fsdp"),
        P(None, "fsdp", "tp"),
        P("fsdp", None, "tp"),
        P("fsdp", None, "tp"),
        P(None, None, "tp"),
        P(None, "tp"),
        P(("fsdp", "tp"), None),
        P(None, "fsdp", "tp"),
    )
    return jax.shard_map(
        body,
        mesh=mesh,
        in_specs=placed,
        out_specs=(P(None, "fsdp", "tp"), P(None, None, "fsdp", "tp")),
        check_vma=False,
    )
```

time: 32.9 us -> 31.2 us (0.948)
  Pallas kernels: 32.1 us -> 30.4 us
    pallas_call x1, Pallas kernels: 31.5 us -> 29.7 us  [body(): pl.pallas_call(kernel, out_shape=(pltpu.VMEM(queries.shape, BF16), pltpu....]
where the time goes in v3:
time: 31.2 us; the launch traced here: 31 us
  Pallas kernels  30.4 us (97%)
  between operations  0.64 us (2%)
    pallas_call x1, Pallas kernels, body(): pl.pallas_call(kernel, out_shape=(pltpu.VMEM(queries.shape, BF16), pltpu....  29.7 us
    pallas_call x1, Pallas kernels, body(): pl.pallas_call(deliver, out_shape=(jax.ShapeDtypeStruct(queries.shape, BF...  0.64 us

profile of v3, /device:TPU:1, one launch (start us, length us, event | category | flops | bytes accessed | tf_op | source)
XLA Modules:
  0.0 31.0 jit_solution(17931333350212666590)
XLA Ops:
  0.6 29.7 %adapter_attention.1 = (bf16[3,8,1024]{2,1,0:T(8,128)(2,1)S(1)}, bf16[2,3,8,128]{3,2,1,0:T(8,128)(2,1)S(1)}) custom-call(bf16[3,8,8192]{2,1,0:T(8,128)(2,1)} %x_hbm.1, s32[8]{0:T(128)} %len_hbm.1, bf16[3,8,1024]{2,1,0:T(8,128)(2,1)} %q_hbm.1, bf16[8,64,128]{2,1,0:T(8,128)(2,1)} %k_hbm.1, bf16[8,64,128]{2,1,0:T(8,128)(2,1)} %v_hbm.1, ...), custom_call_target="tpu_custom_call" | custom-call | tf_op jit(solution)/shard_map/adapter_attention/pallas_call | solution.py:470
  30.4 0.6 %deliver.1 = (bf16[3,8,1024]{2,1,0:T(8,128)(2,1)}, bf16[2,3,8,128]{3,2,1,0:T(8,128)(2,1)}) custom-call(bf16[3,8,1024]{2,1,0:T(8,128)(2,1)S(1)} %get-tuple-element.4.att_v, bf16[2,3,8,128]{3,2,1,0:T(8,128)(2,1)S(1)} %get-tuple-element.5.ent_v), custom_call_target="tpu_custom_call" | custom-call | tf_op jit(solution)/shard_map/deliver/pallas_call | solution.py:526

commit v4 on v3

--- a/solution.py
+++ b/solution.py
@@ -70,6 +70,7 @@
     d_all,
     xs,
     xr,
+    x_all,
     u1,
     u2,
     pp,
@@ -100,8 +101,10 @@
     p_recv,
     t_send,
     t_recv,
-    near_in,
-    go,
+    near_x,
+    near_t,
+    go_x,
+    go_t,
 ):
     f = lax.axis_index("fsdp")
     t = lax.axis_index("tp")
@@ -117,9 +120,7 @@
         return lax.rem(i + d, n)
 
     def load(i, src, dst):
-        copy = pltpu.make_async_copy(src, dst, in_sem.at[i])
-        copy.start()
-        return copy
+        return pltpu.make_async_copy(src, dst, in_sem.at[i])
 
     loads = {
         "u": load(0, u_hbm, u_v),
@@ -173,8 +174,11 @@
     def u2_copy(d, block):
         return along_x(u2.at[block], u2.at[block], u2_send, u2_recv, d)
 
-    def t_copy(d, block):
-        return remote(pt.at[block], pt.at[block], t_send.at[d], t_recv.at[d], (f, plus(t, d, NT)))
+    def t_out(to):
+        return remote(pt.at[t], pt.at[t], t_send.at[to], t_recv.at[t], (f, to))
+
+    def t_in(by):
+        return remote(pt.at[by], pt.at[by], t_send.at[by], t_recv.at[by], (f, by))
 
     def from_x(d):
         return plus(x, NX - d, NX)
@@ -200,15 +204,18 @@
         for d in range(1, NT):
             signal(barrier, (f, plus(t, d, NT)))
 
-    pl.semaphore_wait(barrier, jnp.where(half == 0, NY + NX + NT - 3, 2 * NY))
-
     @pl.when(half == 1)
     def _():
+        pl.semaphore_wait(barrier, 2 * NY)
         for yy in Y_ORDER:
             d_out(yy).start()
 
-    @pl.when(half == 0)
-    def _():
+    for copy in loads.values():
+        copy.start()
+
+    @pl.when(half == 0)
+    def _():
+        pl.semaphore_wait(barrier, NY + NX + NT - 3)
         for d in range(1, NY):
             d_out(plus(y, d, NY)).start()
 
@@ -322,42 +329,52 @@
         sine = jnp.sin(angle)
         sin_v[pl.ds(s * ROWS, ROWS)] = jnp.where(lane < turn, -sine, sine)
 
+    def gather_x():
+        x_all[...] = jnp.concatenate(
+            [stack_steps(xr.at[j], slice(None)) for j in range(NX)], axis=0
+        ).astype(BF16)
+
     @pl.when(half == 0)
     def _():
         d_load.wait()
         d_in(q + 1).wait_recv()
         for d in range(1, NX):
-            signal(near_in, (at(y, 0, plus(x, d, NX)), t))
+            signal(near_x, (at(y, 0, plus(x, d, NX)), t))
         for d in range(1, NT):
-            signal(near_in, (f, plus(t, d, NT)))
-        pl.semaphore_wait(near_in, NX + NT - 2)
-        signal(go, (at(y, 1, x), mirror))
+            signal(near_t, (f, plus(t, d, NT)))
+        pl.semaphore_wait(near_x, NX - 1)
+        signal(go_x, (at(y, 1, x), mirror))
+        for d in range(1, NX):
+            x_copy(d, from_x(d)).wait_recv()
+        gather_x()
         for d in range(1, NY):
             d_in(plus(y, d, NY) * 2).wait_recv()
             d_in(plus(y, d, NY) * 2 + 1).wait_recv()
 
     @pl.when(half == 1)
     def _():
-        pl.semaphore_wait(go, 1)
+        pl.semaphore_wait(go_x, 1)
         for d in range(1, NX):
             x_copy(d, x).start()
+        for d in range(1, NX):
+            x_copy(d, from_x(d)).wait_recv()
+        gather_x()
         d_over().wait_recv()
 
-    for d in range(1, NX):
-        x_copy(d, from_x(d)).wait_recv()
-    mine = jnp.concatenate([stack_steps(xr.at[j], slice(None)) for j in range(NX)], axis=0)
-    partial = dot(mine.astype(BF16), d_all[...].reshape(NQ * D_ROWS, HEAD))
+    partial = dot(x_all[...], d_all[...].reshape(NQ * D_ROWS, HEAD))
     for j in range(NX):
         for s in range(STEPS):
             base = j * N + s * ROWS
             pp[j, s] = partial[base : base + ROWS]
-    for d in range(1, NX):
+    for d in (2, 1, 3):
         p_copy(d, x).start()
     pr[x] = pp[x]
 
     @pl.when(half == 0)
     def _():
         d_over().start()
+        pl.semaphore_wait(near_t, NT - 1)
+        signal(go_t, (at(y, 1, x), mirror))
         for d in range(1, NY):
             u1_in(plus(y, d, NY) * 2).wait_recv()
         for yy in range(NY):
@@ -376,8 +393,16 @@
         p_copy(d, from_x(d)).wait_recv()
     for s in range(STEPS):
         pt[t, s] = pr[0, s] + pr[1, s] + pr[2, s] + pr[3, s]
-    for d in range(1, NT):
-        t_copy(d, t).start()
+
+    @pl.when(half == 1)
+    def _():
+        pl.semaphore_wait(go_t, 1)
+
+    for to in range(NT):
+
+        @pl.when(t != to)
+        def _(to=to):
+            t_out(to).start()
 
     for d in range(1, NX):
         u2_copy(d, from_x(d)).wait_recv()
@@ -411,7 +436,7 @@
         u2_copy(d, x).wait_send()
 
     for d in range(1, NT):
-        t_copy(d, from_t(d)).wait_recv()
+        t_in(from_t(d)).wait_recv()
     sums = []
     for s in range(STEPS):
         total = pt[0, s]
@@ -446,7 +471,7 @@
             att_v[s, :, h * HEAD : (h + 1) * HEAD] = out[base : base + ROWS].astype(BF16)
 
     for d in range(1, NT):
-        t_copy(d, t).wait_send()
+        t_out(from_t(d)).wait_send()
 
 
 def deliver(att_v, ent_v, att_hbm, ent_hbm, sem):
@@ -485,6 +510,7 @@
             vmem((NQ, D_ROWS, HEAD), BF16),
             vmem((NX, STEPS, ROWS, NQ * D_ROWS), BF16),
             vmem((NX, STEPS, ROWS, NQ * D_ROWS), BF16),
+            vmem((NX * N, NQ * D_ROWS), BF16),
             vmem((NQ, 1, 2 * HEAD), F32),
             vmem((NX, NQ, 2 * HEAD), BF16),
             vmem((NX, STEPS, ROWS, HEAD), F32),
@@ -517,6 +543,8 @@
             dma((NT,)),
             pltpu.SemaphoreType.REGULAR,
             pltpu.SemaphoreType.REGULAR,
+            pltpu.SemaphoreType.REGULAR,
+            pltpu.SemaphoreType.REGULAR,
         ],
         compiler_params=pltpu.CompilerParams(
             collective_id=0, has_side_effects=True, vmem_limit_bytes=60 * 1024 * 1024

time: 31.2 us -> 29.7 us (0.952)
  Pallas kernels: 30.4 us -> 28.6 us
    pallas_call x1, Pallas kernels: 29.7 us -> 28 us  [body(): pl.pallas_call(kernel, out_shape=(pltpu.VMEM(queries.shape, BF16), pltpu....]
where the time goes in v4:
time: 29.7 us; the launch traced here: 29.3 us
  Pallas kernels  28.6 us (96%)
  between operations  0.64 us (2%)
    pallas_call x1, Pallas kernels, body(): pl.pallas_call(kernel, out_shape=(pltpu.VMEM(queries.shape, BF16), pltpu....  28 us
    pallas_call x1, Pallas kernels, body(): pl.pallas_call(deliver, out_shape=(jax.ShapeDtypeStruct(queries.shape, BF...  0.64 us

profile of v4, /device:TPU:1, one launch (start us, length us, event | category | flops | bytes accessed | tf_op | source)
XLA Modules:
  0.0 29.3 jit_solution(4318516453992654334)
XLA Ops:
  0.6 28.0 %adapter_attention.1 = (bf16[3,8,1024]{2,1,0:T(8,128)(2,1)S(1)}, bf16[2,3,8,128]{3,2,1,0:T(8,128)(2,1)S(1)}) custom-call(bf16[3,8,8192]{2,1,0:T(8,128)(2,1)} %x_hbm.1, s32[8]{0:T(128)} %len_hbm.1, bf16[3,8,1024]{2,1,0:T(8,128)(2,1)} %q_hbm.1, bf16[8,64,128]{2,1,0:T(8,128)(2,1)} %k_hbm.1, bf16[8,64,128]{2,1,0:T(8,128)(2,1)} %v_hbm.1, ...), custom_call_target="tpu_custom_call" | custom-call | tf_op jit(solution)/shard_map/adapter_attention/pallas_call | solution.py:495
  28.6 0.6 %deliver.1 = (bf16[3,8,1024]{2,1,0:T(8,128)(2,1)}, bf16[2,3,8,128]{3,2,1,0:T(8,128)(2,1)}) custom-call(bf16[3,8,1024]{2,1,0:T(8,128)(2,1)S(1)} %get-tuple-element.4.att_v, bf16[2,3,8,128]{3,2,1,0:T(8,128)(2,1)S(1)} %get-tuple-element.5.ent_v), custom_call_target="tpu_custom_call" | custom-call | tf_op jit(solution)/shard_map/deliver/pallas_call | solution.py:554

commit v5 on v4

--- a/solution.py
+++ b/solution.py
@@ -27,6 +27,7 @@
 M = STEPS * GROUP * ROWS
 SLOTS = ROWS * CACHE
 W_PARTS = 8
+T_ORDER = (1, 0, 3, 2, 5, 4, 7, 6)
 Y_ORDER = (0, 1, 2, 3, 7, 6, 5, 4)
 
 
@@ -71,8 +72,8 @@
     xs,
     xr,
     x_all,
-    u1,
-    u2,
+    u_all,
+    u_far,
     pp,
     pr,
     pt,
@@ -94,7 +95,10 @@
     x_recv,
     u1_send,
     u1_recv,
-    uf_sem,
+    uh_send,
+    uh_recv,
+    ub_send,
+    ub_recv,
     u2_send,
     u2_recv,
     p_send,
@@ -150,18 +154,34 @@
     def d_in(qq):
         return remote(d_hbm, d_all.at[qq], d_send.at[0], d_recv.at[qq], (f, t))
 
-    def u1_out(yy):
-        return remote(u_own, u1.at[q], u1_send.at[yy], u1_recv.at[q], (at(yy, 0, x), t))
-
-    def u1_in(qq):
-        return remote(u_own, u1.at[qq], u1_send.at[0], u1_recv.at[qq], (f, t))
+    def u_out(yy):
+        where = (at(yy, 0, x), t)
+        return remote(u_own, u_all.at[x, 0, y], u1_send.at[yy], u1_recv.at[y, 0], where)
+
+    def u_out_over(yy):
+        where = (at(yy, 0, x), mirror)
+        return remote(u_own, u_far.at[y], u1_send.at[yy], u1_recv.at[y, 1], where)
+
+    def u_in(yy):
+        return remote(u_own, u_all.at[x, 0, yy], u1_send.at[0], u1_recv.at[yy, 0], (f, t))
+
+    def u_in_over(yy):
+        return remote(u_own, u_far.at[yy], u1_send.at[0], u1_recv.at[yy, 1], (f, t))
+
+    def u_home(xx):
+        where = (at(y, 0, xx), mirror)
+        return remote(u_far, u_all.at[x, 1], uh_send.at[xx], uh_recv.at[x], where)
+
+    def u_home_in(xx):
+        return remote(u_far, u_all.at[xx, 1], uh_send.at[xx], uh_recv.at[xx], (f, t))
+
+    def u_back(h):
+        source, to = ((u_all.at[x, 0], t), (u_far, mirror))[h]
+        return remote(source, u_all.at[x, h], ub_send.at[h], ub_recv.at[h], (at(y, 1, x), to))
 
     def d_over():
         return remote(d_all, d_all, df_sem.at[0], df_sem.at[1], (at(y, 1 - half, x), mirror))
 
-    def u1_over():
-        return remote(u1, u1, uf_sem.at[0], uf_sem.at[1], (at(y, 1 - half, x), t))
-
     def along_x(src, dst, send, recv, d):
         return remote(src, dst, send.at[d], recv.at[d], (at(y, half, plus(x, d, NX)), t))
 
@@ -171,8 +191,11 @@
     def p_copy(d, block):
         return along_x(pp.at[plus(x, d, NX)], pr.at[block], p_send, p_recv, d)
 
-    def u2_copy(d, block):
-        return along_x(u2.at[block], u2.at[block], u2_send, u2_recv, d)
+    def u2_half(d, block):
+        return along_x(u_all.at[block, 0], u_all.at[block, 0], u2_send, u2_recv, d)
+
+    def u2_both(d, block):
+        return along_x(u_all.at[block], u_all.at[block], u2_send, u2_recv, d)
 
     def t_out(to):
         return remote(pt.at[t], pt.at[t], t_send.at[to], t_recv.at[t], (f, to))
@@ -185,6 +208,8 @@
 
     def from_t(d):
         return plus(t, NT - d, NT)
+
+    loads["u"].start()
 
     barrier = pltpu.get_barrier_semaphore()
 
@@ -196,7 +221,6 @@
         d_load.start()
         for yy in Y_ORDER:
             signal(barrier, (at(yy, 1, x), mirror))
-            signal(barrier, (at(yy, 1, x), t))
         for d in range(1, NY):
             signal(barrier, (at(plus(y, d, NY), 0, x), t))
         for d in range(1, NX):
@@ -206,33 +230,20 @@
 
     @pl.when(half == 1)
     def _():
-        pl.semaphore_wait(barrier, 2 * NY)
+        pl.semaphore_wait(barrier, NY)
         for yy in Y_ORDER:
             d_out(yy).start()
 
-    for copy in loads.values():
-        copy.start()
-
-    @pl.when(half == 0)
-    def _():
-        pl.semaphore_wait(barrier, NY + NX + NT - 3)
-        for d in range(1, NY):
-            d_out(plus(y, d, NY)).start()
-
     loads["u"].wait()
     u_own[...] = jnp.concatenate([u_v[0:1].astype(F32), u_v[1:2].astype(F32)], axis=1)
 
     @pl.when(half == 1)
     def _():
         for yy in Y_ORDER:
-            u1_out(yy).start()
-
-    @pl.when(half == 0)
-    def _():
-        u1[q] = u_own[...]
-        for d in range(1, NY):
-            u1_out(plus(y, d, NY)).start()
-
+            u_out_over(yy).start()
+
+    for name in ("x", "len", "bias", "q", "k", "v"):
+        loads[name].start()
     for i in range(W_PARTS):
         w_load(i).start()
 
@@ -270,8 +281,14 @@
     xr[x] = xs[x]
     @pl.when(half == 0)
     def _():
+        u_all[x, 0, y] = u_own[...]
+        pl.semaphore_wait(barrier, NY + NX + NT - 3)
+        for d in range(1, NY):
+            d_out(plus(y, d, NY)).start()
         for d in range(1, NX):
             x_copy(d, x).start()
+        for d in range(1, NY):
+            u_out(plus(y, d, NY)).start()
 
     for name in ("q", "k", "len"):
         loads[name].wait()
@@ -342,8 +359,6 @@
             signal(near_x, (at(y, 0, plus(x, d, NX)), t))
         for d in range(1, NT):
             signal(near_t, (f, plus(t, d, NT)))
-        pl.semaphore_wait(near_x, NX - 1)
-        signal(go_x, (at(y, 1, x), mirror))
         for d in range(1, NX):
             x_copy(d, from_x(d)).wait_recv()
         gather_x()
@@ -373,21 +388,23 @@
     @pl.when(half == 0)
     def _():
         d_over().start()
-        pl.semaphore_wait(near_t, NT - 1)
-        signal(go_t, (at(y, 1, x), mirror))
+        pl.semaphore_wait(near_x, NX - 1)
+        signal(go_x, (at(y, 1, x), mirror))
         for d in range(1, NY):
-            u1_in(plus(y, d, NY) * 2).wait_recv()
+            u_in(plus(y, d, NY)).wait_recv()
+        for d in range(1, NX):
+            u2_half(d, x).start()
         for yy in range(NY):
-            u1_in(yy * 2 + 1).wait_recv()
-        u1_over().start()
+            u_in_over(yy).wait_recv()
+        for xx in range(NX):
+            u_home(xx).start()
 
     @pl.when(half == 1)
     def _():
-        u1_over().wait_recv()
-
-    u2[x] = u1[...].reshape(NQ, 2 * HEAD).astype(BF16)
-    for d in range(1, NX):
-        u2_copy(d, x).start()
+        for h in range(2):
+            u_back(h).wait_recv()
+        for d in range(1, NX):
+            u2_both(d, x).start()
 
     for d in range(1, NX):
         p_copy(d, from_x(d)).wait_recv()
@@ -398,18 +415,38 @@
     def _():
         pl.semaphore_wait(go_t, 1)
 
-    for to in range(NT):
+    for to in T_ORDER:
 
         @pl.when(t != to)
         def _(to=to):
             t_out(to).start()
 
-    for d in range(1, NX):
-        u2_copy(d, from_x(d)).wait_recv()
+    @pl.when(half == 0)
+    def _():
+        pl.semaphore_wait(near_t, NT - 1)
+        signal(go_t, (at(y, 1, x), mirror))
+        for h in range(2):
+            u_back(h).start()
+
+    @pl.when(half == 0)
+    def _():
+        for d in range(1, NX):
+            u2_half(d, from_x(d)).wait_recv()
+        for xx in range(NX):
+            u_home_in(xx).wait_recv()
+
+    @pl.when(half == 1)
+    def _():
+        for d in range(1, NX):
+            u2_both(d, from_x(d)).wait_recv()
+
     ranks = NQ * NX
     order = iota((ranks, ranks), 0)
-    order = iota((ranks, ranks), 1) == lax.rem(order, NX) * NQ + order // NX
-    up = dot(jnp.where(order, 1.0, 0.0).astype(BF16), u2[...].reshape(ranks, 2 * HEAD))
+    order = iota((ranks, ranks), 1) == (
+        lax.rem(order, NX) * NQ + lax.rem(order // NX, 2) * NY + order // (2 * NX)
+    )
+    rows = u_all[...].reshape(ranks, 2 * HEAD).astype(BF16)
+    up = dot(jnp.where(order, 1.0, 0.0).astype(BF16), rows)
     up = up * ADAPTER_SCALE
     which = iota((ranks, 2 * HEAD), 1) < HEAD
     ublk[...] = jnp.concatenate(
@@ -420,20 +457,26 @@
     def _():
         for d in range(1, NY):
             d_out(plus(y, d, NY)).wait_send()
-            u1_out(plus(y, d, NY)).wait_send()
+            u_out(plus(y, d, NY)).wait_send()
         d_over().wait_send()
-        u1_over().wait_send()
+        for xx in range(NX):
+            u_home(xx).wait_send()
+        for h in range(2):
+            u_back(h).wait_send()
+        for d in range(1, NX):
+            u2_half(d, x).wait_send()
 
     @pl.when(half == 1)
     def _():
         for yy in range(NY):
             d_out(yy).wait_send()
-            u1_out(yy).wait_send()
+            u_out_over(yy).wait_send()
+        for d in range(1, NX):
+            u2_both(d, x).wait_send()
 
     for d in range(1, NX):
         x_copy(d, x).wait_send()
         p_copy(d, x).wait_send()
-        u2_copy(d, x).wait_send()
 
     for d in range(1, NT):
         t_in(from_t(d)).wait_recv()
@@ -511,8 +554,8 @@
             vmem((NX, STEPS, ROWS, NQ * D_ROWS), BF16),
             vmem((NX, STEPS, ROWS, NQ * D_ROWS), BF16),
             vmem((NX * N, NQ * D_ROWS), BF16),
-            vmem((NQ, 1, 2 * HEAD), F32),
-            vmem((NX, NQ, 2 * HEAD), BF16),
+            vmem((NX, 2, NY, 1, 2 * HEAD), F32),
+            vmem((NY, 1, 2 * HEAD), F32),
             vmem((NX, STEPS, ROWS, HEAD), F32),
             vmem((NX, STEPS, ROWS, HEAD), F32),
             vmem((NT, STEPS, ROWS, HEAD), F32),
@@ -533,7 +576,10 @@
             dma((NX,)),
             dma((NX,)),
             dma((NY,)),
-            dma((NQ,)),
+            dma((NY, 2)),
+            dma((NX,)),
+            dma((NX,)),
+            dma((2,)),
             dma((2,)),
             dma((NX,)),
             dma((NX,)),

time: 29.7 us -> 29.4 us (0.990); the launches traced: 29.3 us -> 29.3 us
  no operation moved by 1% of the time
where the time goes in v5:
time: 29.4 us; the launch traced here: 29.3 us
  Pallas kernels  28.6 us (97%)
  between operations  0.64 us (2%)
    pallas_call x1, Pallas kernels, body(): pl.pallas_call(kernel, out_shape=(pltpu.VMEM(queries.shape, BF16), pltpu....  28 us
    pallas_call x1, Pallas kernels, body(): pl.pallas_call(deliver, out_shape=(jax.ShapeDtypeStruct(queries.shape, BF...  0.64 us

profile of v5, /device:TPU:1, one launch (start us, length us, event | category | flops | bytes accessed | tf_op | source)
XLA Modules:
  0.0 29.3 jit_solution(12962997254202892811)
XLA Ops:
  0.6 28.0 %adapter_attention.1 = (bf16[3,8,1024]{2,1,0:T(8,128)(2,1)S(1)}, bf16[2,3,8,128]{3,2,1,0:T(8,128)(2,1)S(1)}) custom-call(bf16[3,8,8192]{2,1,0:T(8,128)(2,1)} %x_hbm.1, s32[8]{0:T(128)} %len_hbm.1, bf16[3,8,1024]{2,1,0:T(8,128)(2,1)} %q_hbm.1, bf16[8,64,128]{2,1,0:T(8,128)(2,1)} %k_hbm.1, bf16[8,64,128]{2,1,0:T(8,128)(2,1)} %v_hbm.1, ...), custom_call_target="tpu_custom_call" | custom-call | tf_op jit(solution)/shard_map/adapter_attention/pallas_call | solution.py:538
  28.6 0.6 %deliver.1 = (bf16[3,8,1024]{2,1,0:T(8,128)(2,1)}, bf16[2,3,8,128]{3,2,1,0:T(8,128)(2,1)}) custom-call(bf16[3,8,1024]{2,1,0:T(8,128)(2,1)S(1)} %get-tuple-element.4.att_v, bf16[2,3,8,128]{3,2,1,0:T(8,128)(2,1)S(1)} %get-tuple-element.5.ent_v), custom_call_target="tpu_custom_call" | custom-call | tf_op jit(solution)/shard_map/deliver/pallas_call | solution.py:600

commit v6 on v5

--- a/solution.py
+++ b/solution.py
@@ -409,7 +409,7 @@
     for d in range(1, NX):
         p_copy(d, from_x(d)).wait_recv()
     for s in range(STEPS):
-        pt[t, s] = pr[0, s] + pr[1, s] + pr[2, s] + pr[3, s]
+        pt[t, s] = (pr[0, s] + pr[1, s] + pr[2, s] + pr[3, s]).astype(BF16)
 
     @pl.when(half == 1)
     def _():
@@ -482,9 +482,9 @@
         t_in(from_t(d)).wait_recv()
     sums = []
     for s in range(STEPS):
-        total = pt[0, s]
+        total = pt[0, s].astype(F32)
         for i in range(1, NT):
-            total = total + pt[i, s]
+            total = total + pt[i, s].astype(F32)
         sums.append(total)
     low_rank = jnp.concatenate(sums, axis=0)
     high = low_rank.astype(BF16).astype(F32)
@@ -558,7 +558,7 @@
             vmem((NY, 1, 2 * HEAD), F32),
             vmem((NX, STEPS, ROWS, HEAD), F32),
             vmem((NX, STEPS, ROWS, HEAD), F32),
-            vmem((NT, STEPS, ROWS, HEAD), F32),
+            vmem((NT, STEPS, ROWS, HEAD), BF16),
             vmem((N, width), F32),
             vmem((N, 2 * HEAD), F32),
             vmem((N, HEAD), F32),

time: 29.4 us -> 29.1 us (0.990)
  Pallas kernels: 28.6 us -> 28.3 us
where the time goes in v6:
time: 29.1 us; the launch traced here: 29 us
  Pallas kernels  28.3 us (97%)
  between operations  0.64 us (2%)
    pallas_call x1, Pallas kernels, body(): pl.pallas_call(kernel, out_shape=(pltpu.VMEM(queries.shape, BF16), pltpu....  27.7 us
    pallas_call x1, Pallas kernels, body(): pl.pallas_call(deliver, out_shape=(jax.ShapeDtypeStruct(queries.shape, BF...  0.64 us

profile of v6, /device:TPU:1, one launch (start us, length us, event | category | flops | bytes accessed | tf_op | source)
XLA Modules:
  0.0 29.0 jit_solution(2221838801703293784)
XLA Ops:
  0.6 27.7 %adapter_attention.1 = (bf16[3,8,1024]{2,1,0:T(8,128)(2,1)S(1)}, bf16[2,3,8,128]{3,2,1,0:T(8,128)(2,1)S(1)}) custom-call(bf16[3,8,8192]{2,1,0:T(8,128)(2,1)} %x_hbm.1, s32[8]{0:T(128)} %len_hbm.1, bf16[3,8,1024]{2,1,0:T(8,128)(2,1)} %q_hbm.1, bf16[8,64,128]{2,1,0:T(8,128)(2,1)} %k_hbm.1, bf16[8,64,128]{2,1,0:T(8,128)(2,1)} %v_hbm.1, ...), custom_call_target="tpu_custom_call" | custom-call | tf_op jit(solution)/shard_map/adapter_attention/pallas_call | solution.py:538
  28.3 0.6 %deliver.1 = (bf16[3,8,1024]{2,1,0:T(8,128)(2,1)}, bf16[2,3,8,128]{3,2,1,0:T(8,128)(2,1)}) custom-call(bf16[3,8,1024]{2,1,0:T(8,128)(2,1)S(1)} %get-tuple-element.4.att_v, bf16[2,3,8,128]{3,2,1,0:T(8,128)(2,1)S(1)} %get-tuple-element.5.ent_v), custom_call_target="tpu_custom_call" | custom-call | tf_op jit(solution)/shard_map/deliver/pallas_call | solution.py:600
